TPU v7x, 512 devices: a whole 4x4x16 slice. The times are simulated.
512 devices in a mesh: grp: 64 (over x, z), dev: 8 (over y, core).
Axes of the slice: x: 4, y: 4, z: 16, core: 2. Of those that a mesh axis runs over, the one named last changes fastest.
Arguments:
- tokens: bfloat16 [32768, 768], P(('grp', 'dev')), may hold values from -6 to 6
- expert_ids: int32 [32768, 8], P(('grp', 'dev')), may hold values from 0 to 511, as said below
- gates: bfloat16 [32768, 8], P(('grp', 'dev')), may hold values from 0.099609375 to 0.5
- w_in: bfloat16 [512, 768, 1536], P(('grp', 'dev')), may hold values from -0.21875 to 0.21875
- w_out: bfloat16 [512, 1536, 768], P(('grp', 'dev')), may hold values from -0.15625 to 0.15625
Outputs:
- mixed: bfloat16 [32768, 768], P(('grp', 'dev'))
Inputs may be any that keep to these rules, and one draw needn't show every extreme that they name: `expert_ids`: row t lists 8 experts; columns 2 * k and 2 * k + 1 are two different experts of one group (experts g * 8 to g * 8 + 7 form group g), and the four groups of a row differ. The owner of token t is t // 64, and its dev index is the owner modulo 8. The tokens of one owner pick one group at most 12 times, and every owner reaches it for some group. The tokens whose owners share a dev index pick each group exactly 4 * 64 times in all and each expert at most 192 times; in every group one expert is picked 192 times by the tokens of every dev index.
All inputs are finite; a program needn't handle non-finite values.
Results may differ from a plain program's by a relative error of at most 0.0057.
Values may be sent and summed in bfloat16 or wider, within the bound.
A program may use at most 64 MiB of HBM per device.

v0:
```python
import jax
import jax.numpy as jnp
from jax import lax
from jax.sharding import PartitionSpec as P


def earlier_count(onehot):
    return jnp.cumsum(onehot, axis=0) - onehot


def contract_rows(left, right):
    return lax.dot_general(
        left,
        right,
        (((0,), (0,)), ((), ())),
        precision=lax.Precision.HIGHEST,
        preferred_element_type=jnp.float32,
    )


def expert_rows(slot_block, w_first, w_second):

    def one_block(rows_block):
        hidden = jnp.maximum(
            jnp.dot(rows_block, w_first, preferred_element_type=jnp.float32), 0.0
        ).astype(jnp.bfloat16)
        return jnp.dot(hidden, w_second, preferred_element_type=jnp.float32).astype(jnp.bfloat16)

    return lax.map(one_block, slot_block)


def seat_sources(seat_of, valid, seat_total):
    item_count = seat_of.shape[0]
    target_seat = jnp.where(valid, seat_of, seat_total)
    empty_seats = jnp.full((seat_total,), item_count, jnp.int32)
    return empty_seats.at[target_seat].set(jnp.arange(item_count, dtype=jnp.int32), mode="drop")


def per_device(tokens, expert_ids, gates, w_in, w_out):
    n_grp = lax.axis_size("grp")
    n_dev = lax.axis_size("dev")
    token_count, feature_width = tokens.shape
    cap_grp = min(token_count, 3 * ((4 * token_count + n_grp - 1) // n_grp))
    cap_exp = min(4 * token_count, 24 * token_count // n_dev)
    seat_total = n_dev * cap_exp
    zero_half = jnp.zeros((), jnp.bfloat16)
    w_first = w_in[0]
    w_second = w_out[0]
    pair_ids = expert_ids.reshape(token_count * 4, 2)
    pair_group = pair_ids[:, 0] // n_dev
    group_hot = (pair_group[:, None] == jnp.arange(n_grp)[None, :]).astype(jnp.int32)
    group_rank = jnp.sum(earlier_count(group_hot) * group_hot, axis=1)
    target = pair_group * cap_grp + group_rank
    slot_count = n_grp * cap_grp
    placed = (target[None, :] == jnp.arange(slot_count)[:, None]).astype(jnp.int32)
    token_hot = placed.reshape(slot_count, token_count, 4).sum(axis=2)
    rows_out = jnp.dot(
        token_hot.astype(jnp.bfloat16), tokens, preferred_element_type=jnp.float32
    ).astype(jnp.bfloat16)
    local_ids = pair_ids % n_dev
    picks_out = jnp.dot(placed, local_ids + 1) - 1
    gains_out = jnp.dot(
        placed.astype(jnp.bfloat16),
        gates.reshape(token_count * 4, 2),
        preferred_element_type=jnp.float32,
    ).astype(jnp.bfloat16)
    rows_in, picks_in, gains_in = (
        lax.all_to_all(
            rows_out.reshape(n_grp, cap_grp, feature_width),
            "grp",
            split_axis=0,
            concat_axis=0,
            tiled=True,
        ),
        lax.all_to_all(
            picks_out.reshape(n_grp, cap_grp, 2), "grp", split_axis=0, concat_axis=0, tiled=True
        ),
        lax.all_to_all(
            gains_out.reshape(n_grp, cap_grp, 2), "grp", split_axis=0, concat_axis=0, tiled=True
        ),
    )
    relay_rows = rows_in.reshape(slot_count, feature_width)
    relay_picks = picks_in.reshape(slot_count, 2)
    relay_gains = gains_in.reshape(slot_count, 2)
    live_count = 4 * token_count
    slot_live = (relay_picks[:, 0] >= 0).astype(jnp.int32)
    slot_order = jnp.cumsum(slot_live) - 1
    packed = (
        (slot_order[None, :] == jnp.arange(live_count)[:, None]) & (slot_live[None, :] > 0)
    ).astype(jnp.int32)
    packed_rows = jnp.dot(
        packed.astype(jnp.bfloat16), relay_rows, preferred_element_type=jnp.float32
    ).astype(jnp.bfloat16)
    packed_picks = jnp.dot(packed, relay_picks)
    packed_gains = jnp.dot(
        packed.astype(jnp.bfloat16), relay_gains, preferred_element_type=jnp.float32
    ).astype(jnp.bfloat16)
    group_rows, group_picks, group_gains = (
        lax.all_gather(packed_rows, "dev", axis=0, tiled=True),
        lax.all_gather(packed_picks, "dev", axis=0, tiled=True),
        lax.all_gather(packed_gains, "dev", axis=0, tiled=True),
    )
    gathered_count = group_rows.shape[0]
    chosen = jnp.sum((group_picks == lax.axis_index("dev")).astype(jnp.int32), axis=1)
    expert_seat = jnp.cumsum(chosen) - 1
    seat_source = seat_sources(expert_seat, chosen > 0, seat_total)
    seat_live = seat_source < gathered_count
    taken_rows = jnp.take(group_rows, jnp.minimum(seat_source, gathered_count - 1), axis=0)
    expert_in = jnp.where(seat_live[:, None], taken_rows, zero_half)
    expert_out = expert_rows(
        expert_in.reshape(n_dev, cap_exp, feature_width), w_first, w_second
    ).reshape(seat_total, feature_width)
    spread_rows = jnp.take(expert_out, jnp.clip(expert_seat, 0, seat_total - 1), axis=0)
    spread = jnp.where((chosen > 0)[:, None], spread_rows, zero_half)
    back = lax.all_to_all(
        spread.reshape(n_dev, live_count, feature_width),
        "dev",
        split_axis=0,
        concat_axis=0,
        tiled=True,
    )
    match = (packed_picks[None, :, :] == jnp.arange(n_dev)[:, None, None]).astype(jnp.float32)
    row_weights = jnp.sum(match * packed_gains.astype(jnp.float32)[None, :, :], axis=2)
    packed_sum = jnp.sum(row_weights[:, :, None] * back.astype(jnp.float32), axis=0)
    partial_value = contract_rows(packed.astype(jnp.float32), packed_sum)
    returned_sums = lax.all_to_all(
        partial_value.reshape(n_grp, cap_grp, feature_width),
        "grp",
        split_axis=0,
        concat_axis=0,
        tiled=True,
    )
    mixed = contract_rows(
        token_hot.astype(jnp.float32), returned_sums.reshape(slot_count, feature_width)
    )
    return mixed.astype(jnp.bfloat16)


def solution(mesh):
    return jax.shard_map(
        per_device,
        mesh=mesh,
        in_specs=(
            P(("grp", "dev"), None),
            P(("grp", "dev"), None),
            P(("grp", "dev"), None),
            P(("grp", "dev"), None, None),
            P(("grp", "dev"), None, None),
        ),
        out_specs=P(("grp", "dev"), None),
        check_vma=False,
    )
```

profile of v0, /device:TPU:6, one launch (start us, length us, event | category | flops | bytes accessed | tf_op | source)
XLA Modules:
  0.0 426.4 jit_solution(9296313556347692572)
XLA Ops:
  6.5 0.8 copy.40
  9.3 0.7 copy.43
  10.0 18.8 %all-to-all-start = ((s32[64,12,2]{1,2,0:T(2,128)}), s32[64,12,2]{1,2,0:T(2,128)S(1)}, u32[]{:S(2)}, u32[]{:S(2)}) async-start(s32[64,12,2]{1,2,0:T(2,128)} %copy.43), calls=%async_computation | async-start | bytes 131072 | tf_op jit(solution)/shard_map/all_to_all | solution.py:75
  29.8 1.3 reshape.303
  31.1 10.6 %all-to-all-done = s32[64,12,2]{1,2,0:T(2,128)S(1)} async-done(((s32[64,12,2]{1,2,0:T(2,128)}), s32[64,12,2]{1,2,0:T(2,128)S(1)}, u32[]{:S(2)}, u32[]{:S(2)}) %all-to-all-start) | async-done | bytes 6176 | tf_op jit(solution)/shard_map/all_to_all | solution.py:75
  41.7 6.4 %all-to-all-start.2 = ((bf16[64,12,768]{2,1,0:T(8,128)(2,1)}), bf16[64,12,768]{2,1,0:T(8,128)(2,1)S(1)}, u32[]{:S(2)}, u32[]{:S(2)}) async-start(bf16[64,12,768]{2,1,0:T(8,128)(2,1)} %reshape.303), calls=%async_computation.2 | async-start | bytes 3145728 | tf_op jit(solution)/shard_map/all_to_all | solution.py:68
  48.9 74.3 %all-to-all-done.2 = bf16[64,12,768]{2,1,0:T(8,128)(2,1)S(1)} async-done(((bf16[64,12,768]{2,1,0:T(8,128)(2,1)}), bf16[64,12,768]{2,1,0:T(8,128)(2,1)S(1)}, u32[]{:S(2)}, u32[]{:S(2)}) %all-to-all-start.2) | async-done | bytes 1179680 | tf_op jit(solution)/shard_map/all_to_all | solution.py:68
  123.5 1.3 convolution_convert_fusion.2
  125.4 0.6 copy.48
  126.0 6.9 %all-to-all-start.1 = ((bf16[64,12,2]{1,2,0:T(2,128)(2,1)}), bf16[64,12,2]{1,2,0:T(2,128)(2,1)S(1)}, u32[]{:S(2)}, u32[]{:S(2)}) async-start(bf16[64,12,2]{1,2,0:T(2,128)(2,1)} %copy.48), calls=%async_computation.1 | async-start | bytes 65536 | tf_op jit(solution)/shard_map/all_to_all | solution.py:78
  133.5 12.1 %all_gather.6 = s32[2048,2]{0,1:T(2,128)S(1)} all-gather(s32[256,2]{0,1:T(2,128)S(1)} %fusion.19), channel_id=1, replica_groups=mesh['grp'=64,'dev'=8] {'dev'}, dimensions={0}, use_global_device_ids=true | all-gather | bytes 18432 | tf_op jit(solution)/shard_map/all_gather | solution.py:100
  146.4 8.0 %scatter_custom_fusion = s32[1536]{0:T(1024)S(1)} fusion(s32[2048]{0:T(1024)S(1)} %bitcast.90, s32[2048]{0:T(1024)S(1)} %iota.29, s32[]{:T(128)} %constant.103.clone.1), kind=kCustom, calls=%fused_computation.109 | custom fusion | bytes 6148 | tf_op jit(solution)/shard_map/scatter | solution.py:36
  154.8 9.0 %gather_fusion = bf16[1536,768]{1,0:T(8,128)(2,1)} fusion(bf16[2048,768]{1,0:T(8,128)(2,1)} %all-gather.2.cloned.1.call-done, s32[2048]{0:T(1024)S(1)} %pad_clamp_fusion), kind=kCustom, calls=%fused_computation | custom fusion | bytes 4724736 | tf_op jit(solution)/shard_map/jit(_take)/gather | solution.py:108
  163.8 3.0 select_select_fusion.1
  166.8 29.7 %while.11 = (s32[]{:T(128)}, bf16[8,192,768]{2,1,0:T(8,128)(2,1)S(1)}, bf16[8,192,768]{2,1,0:T(8,128)(2,1)}, bf16[768,1536]{1,0:T(8,128)(2,1)}, bf16[1536,768]{1,0:T(8,128)(2,1)}) while((s32[]{:T(128)}, bf16[8,192,768]{2,1,0:T(8,128)(2,1)S(1)}, bf16[8,192,768]{2,1,0:T(8,128)(2,1)}, bf16[768,1536]{1,0:T(8,128)(2,1)}, ...), condition=%wide.region_12.13_spmd.clone, body=%wide.region_11.12_spmd.sunk.clone | while | flops 906706944 | bytes 5309509 | solution.py:29
  166.8 3.7 fusion.84
  170.5 3.7 fusion.84
  174.2 3.7 fusion.84
  177.9 3.7 fusion.84
  181.7 3.7 fusion.84
  185.4 3.7 fusion.84
  189.1 3.7 fusion.84
  192.8 3.7 fusion.84
  196.5 9.4 %gather_fusion.1 = bf16[2048,768]{1,0:T(8,128)(2,1)} fusion(bf16[1536,768]{1,0:T(8,128)(2,1)S(1)} %bitcast.82, s32[2048]{0:T(1024)S(1)} %broadcast_clamp_fusion), kind=kCustom, calls=%fused_computation.1 | custom fusion | bytes 6299648 | tf_op jit(solution)/shard_map/jit(_take)/gather | solution.py:113
  205.9 3.5 select_select_fusion
  209.3 3.8 all-to-all-start.3
  214.0 37.3 %all-to-all-done.3 = bf16[8,256,768]{2,1,0:T(8,128)(2,1)S(1)} async-done(((bf16[8,256,768]{2,1,0:T(8,128)(2,1)}), bf16[8,256,768]{2,1,0:T(8,128)(2,1)S(1)}, u32[]{:S(2)}, u32[]{:S(2)}) %all-to-all-start.3) | async-done | bytes 3145760 | tf_op jit(solution)/shard_map/all_to_all | solution.py:115
  252.0 2.2 fusion.12
  254.2 1.4 copy.51
  255.7 158.5 %all_to_all.25 = f32[64,12,768]{2,1,0:T(8,128)S(1)} all-to-all(f32[64,12,768]{2,1,0:T(8,128)S(1)} %copy.51), channel_id=1, replica_groups=mesh['grp'=64,'dev'=8] {'grp'}, dimensions={0} | all-to-all | bytes 4718592 | tf_op jit(solution)/shard_map/all_to_all | solution.py:126
  414.2 1.5 reshape.306
  415.7 3.9 convolution_convert_fusion.3
  (71 shorter events, 7.7 us)
Async XLA Ops:
  6.5 22.8 %copy-start = (bf16[64,768]{1,0:T(8,128)(2,1)S(1)}, bf16[64,768]{1,0:T(8,128)(2,1)}, u32[]{:S(2)}) copy-start(bf16[64,768]{1,0:T(8,128)(2,1)} %param.7) | copy-start | bytes 294916
  10.0 31.7 %all-to-all-start = ((s32[64,12,2]{1,2,0:T(2,128)}), s32[64,12,2]{1,2,0:T(2,128)S(1)}, u32[]{:S(2)}, u32[]{:S(2)}) async-start(s32[64,12,2]{1,2,0:T(2,128)} %copy.43), calls=%async_computation | async-start | bytes 131072 | tf_op jit(solution)/shard_map/all_to_all | solution.py:75
  41.7 81.5 %all-to-all-start.2 = ((bf16[64,12,768]{2,1,0:T(8,128)(2,1)}), bf16[64,12,768]{2,1,0:T(8,128)(2,1)S(1)}, u32[]{:S(2)}, u32[]{:S(2)}) async-start(bf16[64,12,768]{2,1,0:T(8,128)(2,1)} %reshape.303), calls=%async_computation.2 | async-start | bytes 3145728 | tf_op jit(solution)/shard_map/all_to_all | solution.py:68
  48.2 106.7 %all-gather.2.cloned.1.call-start = ((), (), s32[]{:S(2)}) async-start(), calls=%async_computation.5 | async-start | bytes 3538944 | tf_op jit(solution)/shard_map/all_gather | solution.py:99
  48.9 75.8 %copy-start.1 = (bf16[64,8]{0,1:T(8,128)(2,1)S(1)}, bf16[64,8]{0,1:T(8,128)(2,1)}, u32[]{:S(2)}) copy-start(bf16[64,8]{0,1:T(8,128)(2,1)} %param.9) | copy-start | bytes 3076
  126.0 83.3 %all-to-all-start.1 = ((bf16[64,12,2]{1,2,0:T(2,128)(2,1)}), bf16[64,12,2]{1,2,0:T(2,128)(2,1)S(1)}, u32[]{:S(2)}, u32[]{:S(2)}) async-start(bf16[64,12,2]{1,2,0:T(2,128)(2,1)} %copy.48), calls=%async_computation.1 | async-start | bytes 65536 | tf_op jit(solution)/shard_map/all_to_all | solution.py:78
  209.3 42.0 %all-to-all-start.3 = ((bf16[8,256,768]{2,1,0:T(8,128)(2,1)}), bf16[8,256,768]{2,1,0:T(8,128)(2,1)S(1)}, u32[]{:S(2)}, u32[]{:S(2)}) async-start(bf16[8,256,768]{2,1,0:T(8,128)(2,1)} %select_select_fusion), calls=%async_computation.3 | async-start | bytes 6291456 | tf_op jit(solution)/shard_map/all_to_all | solution.py:115
Sparse Core Ops, SparseCore 0:
  124.9 28.0 all-gather.1
where the time goes:
time: 427 us; the launch traced here: 426 us
  blocking collectives  171 us (40%)
  waiting for transfers between devices  122 us (29%)
  matrix products  38.9 us (9%)
  starting transfers between devices  36 us (8%)
  local copies, waits for them, and re-layouts  35.5 us (8%)
  between operations  13.7 us (3%)
  other arithmetic  9.29 us (2%)
    all_to_all x1, blocking collectives, per_device(): lax.all_to_all(partial_value.reshape(n_grp, cap_grp, feature_width), 'grp...  159 us
    all_to_all x1, waiting for transfers between devices, per_device(): lax.all_to_all(rows_out.reshape(n_grp, cap_grp, feature_width), 'grp', sp...  74.3 us
    all_to_all x1, waiting for transfers between devices, per_device(): lax.all_to_all(spread.reshape(n_dev, live_count, feature_width), 'dev', s...  37.3 us
    dot_general x8, matrix products, one_block(): jnp.dot(hidden, w_second, preferred_element_type=jnp.float32)  29.5 us
    all_to_all x1, starting transfers between devices, per_device(): lax.all_to_all(picks_out.reshape(n_grp, cap_grp, 2), 'grp', split_axis=0,...  18.8 us
    all_gather x1, blocking collectives, per_device(): lax.all_gather(packed_picks, 'dev', axis=0, tiled=True)  12.1 us
    all_to_all x1, waiting for transfers between devices, per_device(): lax.all_to_all(picks_out.reshape(n_grp, cap_grp, 2), 'grp', split_axis=0,...  10.6 us
    gather x1, local copies, waits for them, and re-layouts, per_device(): jnp.take(expert_out, jnp.clip(expert_seat, 0, seat_total - 1), axis=0)  9.38 us
  transfers between devices with their start and end apart: 5, of which 3 were waited for; matrix products, arithmetic and copies ran while one was open for 16% of the time, Pallas kernels for 0%

commit v1 on v0

--- a/solution.py
+++ b/solution.py
@@ -2,6 +2,18 @@
 import jax.numpy as jnp
 from jax import lax
 from jax.sharding import PartitionSpec as P
+
+
+def doubled_up(x, axis, dim):
+    ways, here, step = (lax.axis_size(axis), lax.axis_index(axis), x.shape[dim])
+    line, have = (x, 1)
+    while have < ways:
+        line = jnp.concatenate(
+            [line, lax.ppermute(line, axis, [(d, (d - have) % ways) for d in range(ways)])],
+            axis=dim,
+        )
+        have = 2 * have
+    return jnp.roll(line, here * step, axis=dim)
 
 
 def earlier_count(onehot):
@@ -97,7 +109,7 @@
     ).astype(jnp.bfloat16)
     group_rows, group_picks, group_gains = (
         lax.all_gather(packed_rows, "dev", axis=0, tiled=True),
-        lax.all_gather(packed_picks, "dev", axis=0, tiled=True),
+        doubled_up(packed_picks, "dev", 0),
         lax.all_gather(packed_gains, "dev", axis=0, tiled=True),
     )
     gathered_count = group_rows.shape[0]

time: 427 us -> 430 us (level)
  blocking collectives: 171 us -> 159 us
  starting transfers between devices: 36 us -> 43.8 us
  waiting for transfers between devices: 122 us -> 129 us
    all_gather x1 -> x0, blocking collectives: 12.1 us -> none  [per_device(): lax.all_gather(packed_picks, 'dev', axis=0, tiled=True)]
    ppermute x0 -> x3, waiting for transfers between devices: none -> 7.03 us  [doubled_up(): lax.ppermute(line, axis, [(d, (d - have) % ways) for d in range(ways)])]
    ppermute x0 -> x3, starting transfers between devices: none -> 5.68 us  [doubled_up(): lax.ppermute(line, axis, [(d, (d - have) % ways) for d in range(ways)])]
  transfers between devices with their start and end apart: 5 -> 8, of which waited for: 3 -> 5; matrix products, arithmetic and copies ran while one was open for 16% -> 16% of each run, Pallas kernels for 0% -> 0%
where the time goes in v1:
time: 430 us; the launch traced here: 429 us
  blocking collectives  159 us (37%)
  waiting for transfers between devices  129 us (30%)
  starting transfers between devices  43.8 us (10%)
  matrix products  39 us (9%)
  local copies, waits for them, and re-layouts  35.5 us (8%)
  between operations  13.8 us (3%)
  other arithmetic  9.31 us (2%)
    all_to_all x1, blocking collectives, per_device(): lax.all_to_all(partial_value.reshape(n_grp, cap_grp, feature_width), 'grp...  159 us
    all_to_all x1, waiting for transfers between devices, per_device(): lax.all_to_all(rows_out.reshape(n_grp, cap_grp, feature_width), 'grp', sp...  74.3 us
    all_to_all x1, waiting for transfers between devices, per_device(): lax.all_to_all(spread.reshape(n_dev, live_count, feature_width), 'dev', s...  37.3 us
    dot_general x8, matrix products, one_block(): jnp.dot(hidden, w_second, preferred_element_type=jnp.float32)  29.5 us
    all_to_all x1, starting transfers between devices, per_device(): lax.all_to_all(picks_out.reshape(n_grp, cap_grp, 2), 'grp', split_axis=0,...  18.8 us
    all_to_all x1, waiting for transfers between devices, per_device(): lax.all_to_all(picks_out.reshape(n_grp, cap_grp, 2), 'grp', split_axis=0,...  10.6 us
    gather x1, local copies, waits for them, and re-layouts, per_device(): jnp.take(expert_out, jnp.clip(expert_seat, 0, seat_total - 1), axis=0)  9.38 us
    all_to_all x1, starting transfers between devices, per_device(): lax.all_to_all(gains_out.reshape(n_grp, cap_grp, 2), 'grp', split_axis=0,...  9.05 us
  transfers between devices with their start and end apart: 8, of which 5 were waited for; matrix products, arithmetic and copies ran while one was open for 16% of the time, Pallas kernels for 0%

profile of v1, /device:TPU:6, one launch (start us, length us, event | category | flops | bytes accessed | tf_op | source)
XLA Modules:
  0.0 429.3 jit_solution(7352874285917221596)
XLA Ops:
  10.0 18.8 %all-to-all-start = ((s32[64,12,2]{1,2,0:T(2,128)}), s32[64,12,2]{1,2,0:T(2,128)S(1)}, u32[]{:S(2)}, u32[]{:S(2)}) async-start(s32[64,12,2]{1,2,0:T(2,128)} %copy.43), calls=%async_computation | async-start | bytes 131072 | tf_op jit(solution)/shard_map/all_to_all | solution.py:87
  29.8 1.3 reshape.303
  31.1 10.6 %all-to-all-done = s32[64,12,2]{1,2,0:T(2,128)S(1)} async-done(((s32[64,12,2]{1,2,0:T(2,128)}), s32[64,12,2]{1,2,0:T(2,128)S(1)}, u32[]{:S(2)}, u32[]{:S(2)}) %all-to-all-start) | async-done | bytes 6176 | tf_op jit(solution)/shard_map/all_to_all | solution.py:87
  41.7 6.4 %all-to-all-start.2 = ((bf16[64,12,768]{2,1,0:T(8,128)(2,1)}), bf16[64,12,768]{2,1,0:T(8,128)(2,1)S(1)}, u32[]{:S(2)}, u32[]{:S(2)}) async-start(bf16[64,12,768]{2,1,0:T(8,128)(2,1)} %reshape.303), calls=%async_computation.2 | async-start | bytes 3145728 | tf_op jit(solution)/shard_map/all_to_all | solution.py:80
  48.9 74.3 %all-to-all-done.2 = bf16[64,12,768]{2,1,0:T(8,128)(2,1)S(1)} async-done(((bf16[64,12,768]{2,1,0:T(8,128)(2,1)}), bf16[64,12,768]{2,1,0:T(8,128)(2,1)S(1)}, u32[]{:S(2)}, u32[]{:S(2)}) %all-to-all-start.2) | async-done | bytes 1179680 | tf_op jit(solution)/shard_map/all_to_all | solution.py:80
  123.5 1.3 convolution_convert_fusion.2
  126.6 9.0 %all-to-all-start.1 = ((bf16[64,12,2]{1,2,0:T(2,128)(2,1)}), bf16[64,12,2]{1,2,0:T(2,128)(2,1)S(1)}, u32[]{:S(2)}, u32[]{:S(2)}) async-start(bf16[64,12,2]{1,2,0:T(2,128)(2,1)} %copy.48), calls=%async_computation.1 | async-start | bytes 65536 | tf_op jit(solution)/shard_map/all_to_all | solution.py:90
  135.7 2.8 collective-permute-start.1
  138.5 2.8 collective-permute-done.1
  141.3 2.9 collective-permute-start.2
  144.2 4.3 collective-permute-done.2
  149.4 8.0 %scatter_custom_fusion = s32[1536]{0:T(1024)S(1)} fusion(s32[2048]{0:T(1024)S(1)} %bitcast.90, s32[2048]{0:T(1024)S(1)} %iota.29, s32[]{:T(128)} %constant.118.clone.1), kind=kCustom, calls=%fused_computation.119 | custom fusion | bytes 6148 | tf_op jit(solution)/shard_map/scatter | solution.py:48
  157.7 9.0 %gather_fusion = bf16[1536,768]{1,0:T(8,128)(2,1)} fusion(bf16[2048,768]{1,0:T(8,128)(2,1)} %all-gather.2.cloned.1.call-done, s32[2048]{0:T(1024)S(1)} %pad_clamp_fusion), kind=kCustom, calls=%fused_computation | custom fusion | bytes 4724736 | tf_op jit(solution)/shard_map/jit(_take)/gather | solution.py:120
  166.7 3.0 select_select_fusion.1
  169.7 29.7 %while.11 = (s32[]{:T(128)}, bf16[8,192,768]{2,1,0:T(8,128)(2,1)S(1)}, bf16[8,192,768]{2,1,0:T(8,128)(2,1)}, bf16[768,1536]{1,0:T(8,128)(2,1)}, bf16[1536,768]{1,0:T(8,128)(2,1)}) while((s32[]{:T(128)}, bf16[8,192,768]{2,1,0:T(8,128)(2,1)S(1)}, bf16[8,192,768]{2,1,0:T(8,128)(2,1)}, bf16[768,1536]{1,0:T(8,128)(2,1)}, ...), condition=%wide.region_12.13_spmd.clone, body=%wide.region_11.12_spmd.sunk.clone | while | flops 906706944 | bytes 5309509 | solution.py:41
  169.7 3.7 fusion.84
  173.4 3.7 fusion.84
  177.1 3.7 fusion.84
  180.8 3.7 fusion.84
  184.6 3.7 fusion.84
  188.3 3.7 fusion.84
  192.0 3.7 fusion.84
  195.7 3.7 fusion.84
  199.4 9.4 %gather_fusion.1 = bf16[2048,768]{1,0:T(8,128)(2,1)} fusion(bf16[1536,768]{1,0:T(8,128)(2,1)S(1)} %bitcast.82, s32[2048]{0:T(1024)S(1)} %broadcast_clamp_fusion), kind=kCustom, calls=%fused_computation.1 | custom fusion | bytes 6299648 | tf_op jit(solution)/shard_map/jit(_take)/gather | solution.py:125
  208.8 3.5 select_select_fusion
  212.2 3.8 all-to-all-start.3
  216.9 37.3 %all-to-all-done.3 = bf16[8,256,768]{2,1,0:T(8,128)(2,1)S(1)} async-done(((bf16[8,256,768]{2,1,0:T(8,128)(2,1)}), bf16[8,256,768]{2,1,0:T(8,128)(2,1)S(1)}, u32[]{:S(2)}, u32[]{:S(2)}) %all-to-all-start.3) | async-done | bytes 3145760 | tf_op jit(solution)/shard_map/all_to_all | solution.py:127
  254.9 2.2 fusion.12
  257.1 1.4 copy.51
  258.6 158.5 %all_to_all.25 = f32[64,12,768]{2,1,0:T(8,128)S(1)} all-to-all(f32[64,12,768]{2,1,0:T(8,128)S(1)} %copy.51), channel_id=1, replica_groups=mesh['grp'=64,'dev'=8] {'grp'}, dimensions={0} | all-to-all | bytes 4718592 | tf_op jit(solution)/shard_map/all_to_all | solution.py:138
  417.1 1.5 reshape.306
  418.7 3.9 convolution_convert_fusion.3
  (85 shorter events, 9.9 us)
Async XLA Ops:
  6.5 22.8 %copy-start = (bf16[64,768]{1,0:T(8,128)(2,1)S(1)}, bf16[64,768]{1,0:T(8,128)(2,1)}, u32[]{:S(2)}) copy-start(bf16[64,768]{1,0:T(8,128)(2,1)} %param.7) | copy-start | bytes 294916
  10.0 31.7 %all-to-all-start = ((s32[64,12,2]{1,2,0:T(2,128)}), s32[64,12,2]{1,2,0:T(2,128)S(1)}, u32[]{:S(2)}, u32[]{:S(2)}) async-start(s32[64,12,2]{1,2,0:T(2,128)} %copy.43), calls=%async_computation | async-start | bytes 131072 | tf_op jit(solution)/shard_map/all_to_all | solution.py:87
  41.7 81.5 %all-to-all-start.2 = ((bf16[64,12,768]{2,1,0:T(8,128)(2,1)}), bf16[64,12,768]{2,1,0:T(8,128)(2,1)S(1)}, u32[]{:S(2)}, u32[]{:S(2)}) async-start(bf16[64,12,768]{2,1,0:T(8,128)(2,1)} %reshape.303), calls=%async_computation.2 | async-start | bytes 3145728 | tf_op jit(solution)/shard_map/all_to_all | solution.py:80
  48.2 109.6 %all-gather.2.cloned.1.call-start = ((), (), s32[]{:S(2)}) async-start(), calls=%async_computation.5 | async-start | bytes 3538944 | tf_op jit(solution)/shard_map/all_gather | solution.py:111
  48.9 75.8 %copy-start.1 = (bf16[64,8]{0,1:T(8,128)(2,1)S(1)}, bf16[64,8]{0,1:T(8,128)(2,1)}, u32[]{:S(2)}) copy-start(bf16[64,8]{0,1:T(8,128)(2,1)} %param.9) | copy-start | bytes 3076
  125.5 10.1 %collective-permute-start = (s32[256,2]{0,1:T(2,128)S(1)}, s32[256,2]{0,1:T(2,128)S(1)}, u32[]{:S(2)}, u32[]{:S(2)}) collective-permute-start(s32[256,2]{0,1:T(2,128)S(1)} %get-tuple-element.50), channel_id=1, source_target_pairs={{0,7},{1,0},{2,1},{3,2},{4,3},{5,4},{6,5},{7,6},{8,15},{9,8},{10,9... | collective-permute-start | bytes 6152 | tf_op jit(solution)/shard_map/ppermute | solution.py:12
  126.6 85.7 %all-to-all-start.1 = ((bf16[64,12,2]{1,2,0:T(2,128)(2,1)}), bf16[64,12,2]{1,2,0:T(2,128)(2,1)S(1)}, u32[]{:S(2)}, u32[]{:S(2)}) async-start(bf16[64,12,2]{1,2,0:T(2,128)(2,1)} %copy.48), calls=%async_computation.1 | async-start | bytes 65536 | tf_op jit(solution)/shard_map/all_to_all | solution.py:90
  135.7 5.6 %collective-permute-start.1 = (s32[512,2]{0,1:T(2,128)S(1)}, s32[512,2]{0,1:T(2,128)S(1)}, u32[]{:S(2)}, u32[]{:S(2)}) collective-permute-start(s32[512,2]{0,1:T(2,128)S(1)} %pad_add_fusion.1), channel_id=1, source_target_pairs={{0,6},{1,7},{2,0},{3,1},{4,2},{5,3},{6,4},{7,5},{8,14},{9,15},{10,... | collective-permute-start | bytes 12296 | tf_op jit(solution)/shard_map/ppermute | solution.py:12
  141.3 7.2 %collective-permute-start.2 = (s32[1024,2]{0,1:T(2,128)S(1)}, s32[1024,2]{0,1:T(2,128)S(1)}, u32[]{:S(2)}, u32[]{:S(2)}) collective-permute-start(s32[1024,2]{0,1:T(2,128)S(1)} %pad_add_fusion), channel_id=1, source_target_pairs={{0,4},{1,5},{2,6},{3,7},{4,0},{5,1},{6,2},{7,3},{8,12},{9,13},{10,... | collective-permute-start | bytes 24584 | tf_op jit(solution)/shard_map/ppermute | solution.py:12
  212.2 42.0 %all-to-all-start.3 = ((bf16[8,256,768]{2,1,0:T(8,128)(2,1)}), bf16[8,256,768]{2,1,0:T(8,128)(2,1)S(1)}, u32[]{:S(2)}, u32[]{:S(2)}) async-start(bf16[8,256,768]{2,1,0:T(8,128)(2,1)} %select_select_fusion), calls=%async_computation.3 | async-start | bytes 6291456 | tf_op jit(solution)/shard_map/all_to_all | solution.py:127
Sparse Core Ops, SparseCore 0:
  124.9 28.1 all-gather.1
